TPU v7x, 512 devices: a whole 4x8x8 slice. The times are simulated.
512 devices in a mesh: expert: 8 (over z_lo, core), dp: 64 (over x, y, z_hi).
Axes of the slice: x: 4, y: 8, z: 8 (z_hi: 2, z_lo: 4; z = z_hi * 4 + z_lo), core: 2. Of those that a mesh axis runs over, the one named last changes fastest.
Arguments:
- features: bfloat16 [65536, 512], P(('expert', 'dp')), may hold values from -31 to 31
- gradients: bfloat16 [65536, 512], P(('expert', 'dp')), may hold values from -31 to 31
- route_ids: int32 [65536, 2], P(('expert', 'dp')), may hold values from 0 to 7, all different within a row; in each aligned block of 128 rows (0 to 127, 128 to 255, ...) at most 64 rows name the same one
- gate_share: float32 [65536], P(('expert', 'dp')), may hold values from 0.5 to 0.95
- token_mask: int32 [65536], P(('expert', 'dp')), may hold values 0 or 1
- damping: float32 [8, 2, 1], P('expert'), may hold values from 0.5 to 2
Outputs:
- act_inverse: float32 [8, 1, 512, 512], P(None, None, 'dp')
- grad_inverse: float32 [8, 1, 512, 512], P(None, None, 'dp')
Inputs may be any that keep to these rules, and one draw needn't show every extreme that they name: `route_ids`: each token names two different experts. Among the 128 tokens of one device no expert is named by more than 64 tokens, a bound that some block reaches.
All inputs are finite; a program needn't handle non-finite values. Where the computation divides by a largest or mean magnitude, that divisor is 1e-20 or more. No bound on the sum of `token_mask` on one device may be relied on, other than what follows from the above.
Results may differ from a plain program's by a relative error of at most 0.0003.
Values may be sent and summed in bfloat16 or wider, within the bound.
A program may use at most 64 MiB of HBM per device.

v0:
```python
import jax
import jax.numpy as jnp
from jax import lax
from jax.sharding import PartitionSpec as P

EXPERTS = 8
TOP = 2
BLOCK = 512
NBLK = 1
CAP = 64
WIDTH = 512


def padded_to(lines, devices):
    spare = -len(lines) % devices
    return jnp.pad(lines, [(0, spare)] + [(0, 0)] * (lines.ndim - 1))


def in_order(parts, dim):
    parts = jnp.moveaxis(parts, 0, dim)
    dims = parts.shape
    return parts.reshape(*dims[:dim], dims[dim] * dims[dim + 1], *dims[dim + 2 :])


def sent_to_all(value, axis):
    copies = jnp.broadcast_to(value, (lax.axis_size(axis), *value.shape))
    return lax.all_to_all(copies, axis, split_axis=0, concat_axis=0, tiled=True)


def gathered_copies(value, axis, dim):
    return in_order(sent_to_all(value, axis), dim)


def in_blocks(value, dim, devices):
    dims = value.shape
    parts = value.reshape(*dims[:dim], devices, dims[dim] // devices, *dims[dim + 1 :])
    return jnp.moveaxis(parts, dim, 0)


def sent_and_summed(value, axis, dim):
    devices = lax.axis_size(axis)
    parts = lax.all_to_all(in_blocks(value, dim, devices), axis, 0, 0, tiled=True)
    return jnp.sum(parts, axis=0)


def total_of(value, axes):
    padded = padded_to(value, lax.axis_size(axes))
    whole = gathered_copies(sent_and_summed(padded, axes, 0), axes, 0)
    return lax.slice_in_dim(whole, 0, len(value)).reshape(value.shape)


def packed_total(arrays, axis):
    ravelled, at, finished = (jnp.concatenate([a.reshape(-1) for a in arrays]), 0, [])
    so_far = total_of(ravelled, axis)
    for a in arrays:
        finished.append(so_far[at : at + a.size].reshape(a.shape))
        at += a.size
    return tuple(finished)


def in_one_piece(arrays, axis, dim, along):
    both = jnp.concatenate(arrays, axis=along)
    whole, at, finished = (lax.all_gather(both, axis, axis=dim, tiled=True), 0, [])
    for a in arrays:
        finished.append(lax.slice_in_dim(whole, at, at + a.shape[along], axis=along))
        at += a.shape[along]
    return tuple(finished)


def slot_table(route_ids, capacity):
    pair_experts = route_ids.reshape(-1)
    onehot = (pair_experts[:, None] == jnp.arange(EXPERTS, dtype=jnp.int32)[None, :]).astype(
        jnp.int32
    )
    running = jnp.cumsum(onehot, axis=0)
    position = jnp.sum(onehot * running, axis=1) - 1
    target = pair_experts * capacity + position
    sources = jnp.arange(1, pair_experts.shape[0] + 1, dtype=jnp.int32)
    return jnp.zeros((EXPERTS * capacity,), jnp.int32).at[target].set(sources)


def newton_rows(rows_now, matrix, whole_now):
    left_product = jnp.einsum("eirk,eikc->eirc", rows_now, matrix, precision=lax.Precision.HIGHEST)
    return 2.0 * rows_now - jnp.einsum(
        "eirk,eikc->eirc", left_product, whole_now, precision=lax.Precision.HIGHEST
    )


def first_iterate(matrix, identity, inverse_bound):
    bound_scale = inverse_bound[:, :, None, None]
    return 2.0 * bound_scale * identity - bound_scale * bound_scale * matrix


def fold_pack(blocks_full, half):
    corner = blocks_full[:, :, :half, half:]
    upper_left = blocks_full[:, :, :half, :half]
    lower_right = jnp.swapaxes(blocks_full[:, :, half:, half:], 2, 3)
    zero_row = jnp.zeros(blocks_full.shape[:2] + (1, half), jnp.float32)
    top_part = jnp.concatenate([upper_left, zero_row], axis=2)
    low_part = jnp.concatenate([zero_row, lower_right], axis=2)
    row_ids = lax.broadcasted_iota(jnp.int32, (half + 1, half), 0)
    col_ids = lax.broadcasted_iota(jnp.int32, (half + 1, half), 1)
    folded = jnp.where(row_ids <= col_ids, top_part, low_part)
    return (corner, folded)


def fold_unpack(corner, folded, half):
    row_ids = lax.broadcasted_iota(jnp.int32, (half, half), 0)
    col_ids = lax.broadcasted_iota(jnp.int32, (half, half), 1)
    head = folded[:, :, :half, :]
    upper_left = jnp.where(row_ids <= col_ids, head, jnp.swapaxes(head, 2, 3))
    tail = folded[:, :, 1:, :]
    lower_right = jnp.where(row_ids >= col_ids, tail, jnp.swapaxes(tail, 2, 3))
    top_rows = jnp.concatenate([upper_left, corner], axis=3)
    low_rows = jnp.concatenate([jnp.swapaxes(corner, 2, 3), lower_right], axis=3)
    return jnp.concatenate([top_rows, low_rows], axis=2)


def on_device(features, gradients, route_ids, gate_share, token_mask, damping):
    tokens_here = features.shape[0]
    capacity = CAP
    blocks = 2 * NBLK
    kept_mask = token_mask.astype(jnp.float32)
    weight_pair = jnp.stack([gate_share, 1.0 - gate_share], axis=1) * kept_mask[:, None]
    kept_rows = features * token_mask.astype(jnp.bfloat16)[:, None]
    pair_grads = (gradients[:, None, :].astype(jnp.float32) * weight_pair[:, :, None]).astype(
        jnp.bfloat16
    )
    repeated = jnp.broadcast_to(kept_rows[:, None, :], pair_grads.shape)
    pair_rows = jnp.concatenate([repeated, pair_grads], axis=2).reshape(
        tokens_here * TOP, 2 * WIDTH
    )
    padded = jnp.concatenate([jnp.zeros((1, 2 * WIDTH), jnp.bfloat16), pair_rows], axis=0)
    buffer = jnp.take(padded, slot_table(route_ids, capacity), axis=0).reshape(
        EXPERTS, capacity, blocks, BLOCK
    )
    load_inverse = 1.0 / (
        tokens_here * lax.axis_size("expert") * lax.axis_size("dp") * TOP / EXPERTS
    )
    received = lax.all_to_all(buffer, "expert", split_axis=0, concat_axis=1, tiled=True)
    gram_blocks = (
        jnp.einsum("erib,eric->eibc", received, received, preferred_element_type=jnp.float32)
        * load_inverse
    )
    damping_flat = damping.reshape(damping.shape[0], blocks)[:, :, None, None]
    rows_share = BLOCK // lax.axis_size("dp")
    row_start = lax.axis_index("dp") * rows_share
    identity = jnp.eye(BLOCK, dtype=jnp.float32)
    half = BLOCK // 2
    corner, folded = fold_pack(gram_blocks, half)
    corner_sum, folded_sum = packed_total((corner, folded), "dp")
    summed = fold_unpack(corner_sum, folded_sum, half)
    matrix = summed + damping_flat * identity
    largest_sum = jnp.max(jnp.sum(jnp.abs(matrix), axis=3), axis=2)
    inverse_bound = 1.0 / largest_sum
    iterate_one = first_iterate(matrix, identity, inverse_bound)
    iterate_two = newton_rows(iterate_one, matrix, iterate_one)
    second_rows = lax.dynamic_slice_in_dim(iterate_two, row_start, rows_share, 2)
    third_rows = newton_rows(second_rows, matrix, iterate_two)
    act_rows = third_rows[:, :NBLK]
    grad_rows = third_rows[:, NBLK:]
    act_inverse, grad_inverse = in_one_piece((act_rows, grad_rows), "expert", 0, 1)
    return (act_inverse, grad_inverse)


def solution(mesh):
    placed = (
        P(("expert", "dp"), None),
        P(("expert", "dp"), None),
        P(("expert", "dp"), None),
        P(("expert", "dp")),
        P(("expert", "dp")),
        P("expert", None, None),
    )
    return jax.shard_map(
        on_device,
        mesh=mesh,
        in_specs=placed,
        out_specs=(P(None, None, "dp", None), P(None, None, "dp", None)),
        check_vma=False,
    )
```

profile of v0, /device:TPU:1, one launch (start us, length us, event | category | flops | bytes accessed | tf_op | source)
XLA Modules:
  0.0 180.9 jit_solution(5684483519095609114)
XLA Ops:
  0.6 0.8 copy.57
  1.7 0.7 broadcast_multiply_fusion.1
  3.6 1.4 scatter_custom_fusion
  5.1 0.7 fusion.24
  6.1 0.7 subtract_bitcast_fusion
  6.7 0.7 pad_maximum_fusion.1
  7.6 1.0 mul.169
  9.7 2.1 %gather_fusion = bf16[512,1024]{1,0:T(8,128)(2,1)S(1)} fusion(bf16[257,1024]{1,0:T(8,128)(2,1)S(1)} %fusion.13, s32[1024]{0:T(1024)S(1)} %pad_clamp_fusion), kind=kCustom, calls=%fused_computation | custom fusion | bytes 2099200 | tf_op jit(solution)/shard_map/jit(_take)/gather | solution.py:134
  11.7 0.8 gather.7
  12.6 1.2 copy_select_fusion
  13.8 10.3 %all-to-all-start = ((bf16[8,64,2,512]{3,1,2,0:T(8,128)(2,1)}), bf16[8,64,2,512]{3,1,2,0:T(8,128)(2,1)S(1)}, u32[]{:S(2)}, u32[]{:S(2)}) async-start(bf16[8,64,2,512]{3,1,2,0:T(8,128)(2,1)} %copy_select_fusion), calls=%async_computation | async-start | bytes 2097152 | tf_op jit(solution)/shard_map/all_to_all | solution.py:140
  24.2 25.7 %all-to-all-done = bf16[8,64,2,512]{3,1,2,0:T(8,128)(2,1)S(1)} async-done(((bf16[8,64,2,512]{3,1,2,0:T(8,128)(2,1)}), bf16[8,64,2,512]{3,1,2,0:T(8,128)(2,1)S(1)}, u32[]{:S(2)}, u32[]{:S(2)}) %all-to-all-start) | async-done | bytes 1048608 | tf_op jit(solution)/shard_map/all_to_all | solution.py:140
  50.0 0.8 multiply_bitcast_fusion
  52.0 1.4 all_to_all.18
  53.4 45.6 %all_to_all.24 = f32[64,1,4104]{2,1,0:T(1,128)S(1)} all-to-all(f32[64,1,4104]{2,1,0:T(1,128)S(1)} %all_to_all.18), channel_id=1, replica_groups=mesh['expert'=8,'dp'=64] {'dp'}, dimensions={0} | all-to-all | bytes 2101248 | tf_op jit(solution)/shard_map/all_to_all | solution.py:42
  99.6 1.5 broadcast_in_dim.56
  101.2 8.0 %all-to-all-start.2 = ((f32[64,1,4104]{2,1,0:T(1,128)}), f32[64,1,4104]{2,1,0:T(1,128)S(1)}, u32[]{:S(2)}, u32[]{:S(2)}) async-start(f32[64,1,4104]{2,1,0:T(1,128)} %broadcast_in_dim.56), calls=%async_computation.2 | async-start | bytes 2162688 | tf_op jit(solution)/shard_map/all_to_all | solution.py:27
  109.3 31.0 %all-to-all-done.2 = f32[64,1,4104]{2,1,0:T(1,128)S(1)} async-done(((f32[64,1,4104]{2,1,0:T(1,128)}), f32[64,1,4104]{2,1,0:T(1,128)S(1)}, u32[]{:S(2)}, u32[]{:S(2)}) %all-to-all-start.2) | async-done | bytes 1050656 | tf_op jit(solution)/shard_map/all_to_all | solution.py:27
  140.4 2.6 %reduce.5 = f32[64,4104]{1,0:T(8,128)S(1)} reduce(f32[64,1,4104]{2,1,0:T(1,128)S(1)} %all-to-all-done.2, f32[]{:T(128)} %constant.67), dimensions={1}, to_apply=%all_to_all.20.reduce_sub_computation | reduce | bytes 2101252 | tf_op jit(solution)/shard_map/all_to_all | solution.py:27
  143.5 0.9 copy-done.3
  144.5 0.9 fusion.22
  145.4 1.2 copy.74
  146.7 1.0 copy.75
  147.9 1.0 copy.70
  148.9 1.2 bitcast_select_fusion.1
  150.1 1.3 maximum_bitcast_fusion
  152.1 4.1 %fusion.3 = f32[2,512,512]{2,1,0:T(8,128)S(1)} fusion(f32[2]{0:T(128)S(1)} %mul.187, f32[512,512]{1,0:T(8,128)S(1)} %fusion.12, f32[2]{0:T(128)S(1)} %get-tuple-element.2, f32[2,256,512]{2,1,0:T(8,128)S(1)} %get-tuple-element.16, f32[2,256,512]{2,1,0:T(8,128)S(1)} %get-tuple-element.15, f32[2]{0:T(128)S(1)} %bitcast.42), kind=kOutput, calls=%fused_computation.9 | convolution fusion | flops 3225944064 | bytes 5242904 | tf_op jit(solution)/shard_map/eirk,eikc->eirc/dot_general | solution.py:83
  156.2 4.5 %multiply_subtract_fusion = f32[2,512,512]{2,1,0:T(8,128)S(1)} fusion(f32[2,512,512]{2,1,0:T(8,128)S(1)} %fusion.3, f32[2]{0:T(128)S(1)} %mul.187, f32[512,512]{1,0:T(8,128)S(1)} %fusion.12, f32[2]{0:T(128)S(1)} %get-tuple-element.2, f32[2]{0:T(128)S(1)} %bitcast.43, f32[2,256,512]{2,1,0:T(8,128)S(1)} %get-tuple-element.16, ...), kind=kOutput, calls=%fused_computation.6 | convolution fusion | flops 3228565504 | bytes 7340056 | tf_op jit(solution)/shard_map/eirk,eikc->eirc/dot_general | solution.py:84
  160.7 1.3 fusion.14
  162.0 1.1 convolution_subtract_fusion
  163.1 17.1 %all-gather = f32[16,8,512]{2,1,0:T(8,128)S(1)} all-gather(f32[2,8,512]{2,1,0:T(8,128)S(1)} %convolution_subtract_fusion), channel_id=2, replica_groups=mesh['expert'=8,'dp'=64] {'expert'}, dimensions={0}, use_global_device_ids=true | all-gather | bytes 294912 | tf_op jit(solution)/shard_map/all_gather | solution.py:63
  180.2 0.7 fusion.23
  (62 shorter events, 6.5 us)
Async XLA Ops:
  0.6 8.4 %copy-start.4 = (bf16[128,512]{1,0:T(8,128)(2,1)S(1)}, bf16[128,512]{1,0:T(8,128)(2,1)}, u32[]{:S(2)}) copy-start(bf16[128,512]{1,0:T(8,128)(2,1)} %param.6) | copy-start | bytes 393220
  13.8 36.1 %all-to-all-start = ((bf16[8,64,2,512]{3,1,2,0:T(8,128)(2,1)}), bf16[8,64,2,512]{3,1,2,0:T(8,128)(2,1)S(1)}, u32[]{:S(2)}, u32[]{:S(2)}) async-start(bf16[8,64,2,512]{3,1,2,0:T(8,128)(2,1)} %copy_select_fusion), calls=%async_computation | async-start | bytes 2097152 | tf_op jit(solution)/shard_map/all_to_all | solution.py:140
  101.2 39.2 %all-to-all-start.2 = ((f32[64,1,4104]{2,1,0:T(1,128)}), f32[64,1,4104]{2,1,0:T(1,128)S(1)}, u32[]{:S(2)}, u32[]{:S(2)}) async-start(f32[64,1,4104]{2,1,0:T(1,128)} %broadcast_in_dim.56), calls=%async_computation.2 | async-start | bytes 2162688 | tf_op jit(solution)/shard_map/all_to_all | solution.py:27
  143.4 1.0 copy-start.3
  144.5 3.2 %slice-start = ((f32[262656]{0:T(1024)}), f32[131072]{0:T(1024)S(1)}, s32[]{:S(2)}) async-start(f32[262656]{0:T(1024)} %copy-done.3), calls=%async_computation.3 | async-start | bytes 1048576 | tf_op jit(solution)/shard_map/slice | solution.py:56
  147.8 2.2 %copy-start = (f32[1,2,256,256]{3,2,1,0:T(8,128)}, f32[1,2,256,256]{3,2,1,0:T(8,128)S(1)}, u32[]{:S(2)}) copy-start(f32[1,2,256,256]{3,2,1,0:T(8,128)S(1)} %reshape.260) | copy-start | bytes 1572868
  148.9 1.2 copy-start.2
  150.1 1.4 copy-start.1
  150.1 1.4 copy-start.5
where the time goes:
time: 181 us
  blocking collectives  62.7 us (35%)
  waiting for transfers between devices  56.8 us (31%)
  local copies, waits for them, and re-layouts  18.5 us (10%)
  starting transfers between devices  18.3 us (10%)
  other arithmetic  11.9 us (7%)
  matrix products  11.7 us (6%)
    all_to_all x1, blocking collectives, sent_and_summed(): lax.all_to_all(in_blocks(value, dim, devices), axis, 0, 0, tiled=True)  45.6 us
    all_to_all x1, waiting for transfers between devices, sent_to_all(): return lax.all_to_all(copies, axis, split_axis=0, concat_axis=0, tiled=True)  31 us
    all_to_all x1, waiting for transfers between devices, on_device(): lax.all_to_all(buffer, 'expert', split_axis=0, concat_axis=1, tiled=True)  25.7 us
    all_gather x1, blocking collectives, in_one_piece(): lax.all_gather(both, axis, axis=dim, tiled=True)  17.1 us
    all_to_all x1, starting transfers between devices, on_device(): lax.all_to_all(buffer, 'expert', split_axis=0, concat_axis=1, tiled=True)  10.3 us
    all_to_all x1, starting transfers between devices, sent_to_all(): return lax.all_to_all(copies, axis, split_axis=0, concat_axis=0, tiled=True)  7.96 us
    dot_general x2, matrix products, newton_rows(): jnp.einsum('eirk,eikc->eirc', left_product, whole_now, precision=lax.Prec...  5.59 us
    dot_general x2, matrix products, newton_rows(): jnp.einsum('eirk,eikc->eirc', rows_now, matrix, precision=lax.Precision.H...  5.38 us
  transfers between devices with their start and end apart: 2, of which 2 were waited for; matrix products, arithmetic and copies ran while one was open for 0% of the time, Pallas kernels for 0%

commit v1 on v0

--- a/solution.py
+++ b/solution.py
@@ -137,7 +137,12 @@
     load_inverse = 1.0 / (
         tokens_here * lax.axis_size("expert") * lax.axis_size("dp") * TOP / EXPERTS
     )
-    received = lax.all_to_all(buffer, "expert", split_axis=0, concat_axis=1, tiled=True)
+    received = jnp.concatenate(
+        lax.all_to_all(
+            jnp.stack(jnp.split(buffer, lax.axis_size("expert"), axis=0)), "expert", 0, 0
+        ),
+        axis=1,
+    )
     gram_blocks = (
         jnp.einsum("erib,eric->eibc", received, received, preferred_element_type=jnp.float32)
         * load_inverse

time: 181 us -> 186 us (1.028)
  local copies, waits for them, and re-layouts: 18.5 us -> 23.7 us
    unnamed x17 -> x24, local copies, waits for them, and re-layouts: 4.5 us -> 9.15 us
where the time goes in v1:
time: 186 us; the launch traced here: 185 us
  blocking collectives  62.7 us (34%)
  waiting for transfers between devices  56.8 us (31%)
  local copies, waits for them, and re-layouts  23.7 us (13%)
  starting transfers between devices  18.3 us (10%)
  matrix products  11.7 us (6%)
  other arithmetic  10.9 us (6%)
    all_to_all x1, blocking collectives, sent_and_summed(): lax.all_to_all(in_blocks(value, dim, devices), axis, 0, 0, tiled=True)  45.6 us
    all_to_all x1, waiting for transfers between devices, sent_to_all(): return lax.all_to_all(copies, axis, split_axis=0, concat_axis=0, tiled=True)  31 us
    all_to_all x1, waiting for transfers between devices, on_device(): lax.all_to_all(jnp.stack(jnp.split(buffer, lax.axis_size('expert'), axis=...  25.7 us
    all_gather x1, blocking collectives, in_one_piece(): lax.all_gather(both, axis, axis=dim, tiled=True)  17.1 us
    all_to_all x1, starting transfers between devices, on_device(): lax.all_to_all(jnp.stack(jnp.split(buffer, lax.axis_size('expert'), axis=...  10.3 us
    unnamed x24, local copies, waits for them, and re-layouts  9.15 us
    all_to_all x1, starting transfers between devices, sent_to_all(): return lax.all_to_all(copies, axis, split_axis=0, concat_axis=0, tiled=True)  7.96 us
    dot_general x2, matrix products, newton_rows(): jnp.einsum('eirk,eikc->eirc', left_product, whole_now, precision=lax.Prec...  5.59 us
  transfers between devices with their start and end apart: 2, of which 2 were waited for; matrix products, arithmetic and copies ran while one was open for 0% of the time, Pallas kernels for 0%

profile of v1, /device:TPU:1, one launch (start us, length us, event | category | flops | bytes accessed | tf_op | source)
XLA Modules:
  0.0 185.1 jit_solution(5054281868952618223)
XLA Ops:
  0.6 0.8 copy.85
  1.7 0.7 broadcast_multiply_fusion.1
  3.6 1.4 scatter_custom_fusion
  5.1 0.7 fusion.25
  7.6 1.0 mul.169
  9.7 2.1 %gather_fusion = bf16[512,1024]{1,0:T(8,128)(2,1)S(1)} fusion(bf16[257,1024]{1,0:T(8,128)(2,1)S(1)} %fusion.13, s32[1024]{0:T(1024)S(1)} %pad_clamp_fusion), kind=kCustom, calls=%fused_computation | custom fusion | bytes 2099200 | tf_op jit(solution)/shard_map/jit(_take)/gather | solution.py:134
  13.3 0.7 copy_dynamic-update-slice_fusion.6
  14.0 0.7 copy_dynamic-update-slice_fusion.5
  15.3 0.7 copy_dynamic-update-slice_fusion.3
  17.3 0.7 copy_dynamic-update-slice_fusion
  18.0 10.3 %all-to-all-start = ((bf16[8,1,64,2,512]{4,2,3,1,0:T(8,128)(2,1)}), bf16[8,1,64,2,512]{4,2,3,1,0:T(8,128)(2,1)S(1)}, u32[]{:S(2)}, u32[]{:S(2)}) async-start(bf16[8,1,64,2,512]{4,2,3,1,0:T(8,128)(2,1)} %copy_dynamic-update-slice_fusion), calls=%async_computation | async-start | bytes 2097152 | tf_op jit(solution)/shard_map/all_to_all | solution.py:141
  28.4 25.7 %all-to-all-done = bf16[8,1,64,2,512]{4,2,3,1,0:T(8,128)(2,1)S(1)} async-done(((bf16[8,1,64,2,512]{4,2,3,1,0:T(8,128)(2,1)}), bf16[8,1,64,2,512]{4,2,3,1,0:T(8,128)(2,1)S(1)}, u32[]{:S(2)}, u32[]{:S(2)}) %all-to-all-start) | async-done | bytes 1048608 | tf_op jit(solution)/shard_map/all_to_all | solution.py:141
  54.1 0.8 multiply_bitcast_fusion
  56.2 1.4 all_to_all.14
  57.6 45.6 %all_to_all.20 = f32[64,1,4104]{2,1,0:T(1,128)S(1)} all-to-all(f32[64,1,4104]{2,1,0:T(1,128)S(1)} %all_to_all.14), channel_id=1, replica_groups=mesh['expert'=8,'dp'=64] {'dp'}, dimensions={0} | all-to-all | bytes 2101248 | tf_op jit(solution)/shard_map/all_to_all | solution.py:42
  103.8 1.5 broadcast_in_dim.53
  105.4 8.0 %all-to-all-start.2 = ((f32[64,1,4104]{2,1,0:T(1,128)}), f32[64,1,4104]{2,1,0:T(1,128)S(1)}, u32[]{:S(2)}, u32[]{:S(2)}) async-start(f32[64,1,4104]{2,1,0:T(1,128)} %broadcast_in_dim.53), calls=%async_computation.2 | async-start | bytes 2162688 | tf_op jit(solution)/shard_map/all_to_all | solution.py:27
  113.5 31.0 %all-to-all-done.2 = f32[64,1,4104]{2,1,0:T(1,128)S(1)} async-done(((f32[64,1,4104]{2,1,0:T(1,128)}), f32[64,1,4104]{2,1,0:T(1,128)S(1)}, u32[]{:S(2)}, u32[]{:S(2)}) %all-to-all-start.2) | async-done | bytes 1050656 | tf_op jit(solution)/shard_map/all_to_all | solution.py:27
  144.6 2.6 %reduce.5 = f32[64,4104]{1,0:T(8,128)S(1)} reduce(f32[64,1,4104]{2,1,0:T(1,128)S(1)} %all-to-all-done.2, f32[]{:T(128)} %constant.67), dimensions={1}, to_apply=%all_to_all.16.reduce_sub_computation | reduce | bytes 2101252 | tf_op jit(solution)/shard_map/all_to_all | solution.py:27
  147.6 0.9 copy-done.3
  148.7 0.9 fusion.23
  149.6 1.2 copy.109
  150.9 1.0 copy.110
  152.0 1.0 copy.105
  153.1 1.2 bitcast_select_fusion.1
  154.3 1.3 maximum_bitcast_fusion
  156.3 4.1 %fusion.3 = f32[2,512,512]{2,1,0:T(8,128)S(1)} fusion(f32[2]{0:T(128)S(1)} %mul.187, f32[512,512]{1,0:T(8,128)S(1)} %fusion.12, f32[2]{0:T(128)S(1)} %get-tuple-element.2, f32[2,256,512]{2,1,0:T(8,128)S(1)} %get-tuple-element.24, f32[2,256,512]{2,1,0:T(8,128)S(1)} %get-tuple-element.23, f32[2]{0:T(128)S(1)} %bitcast.42), kind=kOutput, calls=%fused_computation.9 | convolution fusion | flops 3225944064 | bytes 5242904 | tf_op jit(solution)/shard_map/eirk,eikc->eirc/dot_general | solution.py:83
  160.4 4.5 %multiply_subtract_fusion = f32[2,512,512]{2,1,0:T(8,128)S(1)} fusion(f32[2,512,512]{2,1,0:T(8,128)S(1)} %fusion.3, f32[2]{0:T(128)S(1)} %mul.187, f32[512,512]{1,0:T(8,128)S(1)} %fusion.12, f32[2]{0:T(128)S(1)} %get-tuple-element.2, f32[2]{0:T(128)S(1)} %bitcast.43, f32[2,256,512]{2,1,0:T(8,128)S(1)} %get-tuple-element.24, ...), kind=kOutput, calls=%fused_computation.6 | convolution fusion | flops 3228565504 | bytes 7340056 | tf_op jit(solution)/shard_map/eirk,eikc->eirc/dot_general | solution.py:84
  164.9 1.3 fusion.14
  166.2 1.1 convolution_subtract_fusion
  167.3 17.1 %all-gather = f32[16,8,512]{2,1,0:T(8,128)S(1)} all-gather(f32[2,8,512]{2,1,0:T(8,128)S(1)} %convolution_subtract_fusion), channel_id=2, replica_groups=mesh['expert'=8,'dp'=64] {'expert'}, dimensions={0}, use_global_device_ids=true | all-gather | bytes 294912 | tf_op jit(solution)/shard_map/all_gather | solution.py:63
  184.4 0.7 fusion.24
  (77 shorter events, 11.3 us)
Async XLA Ops:
  0.6 8.4 %copy-start.4 = (bf16[128,512]{1,0:T(8,128)(2,1)S(1)}, bf16[128,512]{1,0:T(8,128)(2,1)}, u32[]{:S(2)}) copy-start(bf16[128,512]{1,0:T(8,128)(2,1)} %param.6) | copy-start | bytes 393220
  18.0 36.1 %all-to-all-start = ((bf16[8,1,64,2,512]{4,2,3,1,0:T(8,128)(2,1)}), bf16[8,1,64,2,512]{4,2,3,1,0:T(8,128)(2,1)S(1)}, u32[]{:S(2)}, u32[]{:S(2)}) async-start(bf16[8,1,64,2,512]{4,2,3,1,0:T(8,128)(2,1)} %copy_dynamic-update-slice_fusion), calls=%async_computation | async-start | bytes 2097152 | tf_op jit(solution)/shard_map/all_to_all | solution.py:141
  105.4 39.2 %all-to-all-start.2 = ((f32[64,1,4104]{2,1,0:T(1,128)}), f32[64,1,4104]{2,1,0:T(1,128)S(1)}, u32[]{:S(2)}, u32[]{:S(2)}) async-start(f32[64,1,4104]{2,1,0:T(1,128)} %broadcast_in_dim.53), calls=%async_computation.2 | async-start | bytes 2162688 | tf_op jit(solution)/shard_map/all_to_all | solution.py:27
  147.6 1.0 copy-start.3
  148.7 3.2 %slice-start = ((f32[262656]{0:T(1024)}), f32[131072]{0:T(1024)S(1)}, s32[]{:S(2)}) async-start(f32[262656]{0:T(1024)} %copy-done.3), calls=%async_computation.3 | async-start | bytes 1048576 | tf_op jit(solution)/shard_map/slice | solution.py:56
  152.0 2.2 %copy-start = (f32[1,2,256,256]{3,2,1,0:T(8,128)}, f32[1,2,256,256]{3,2,1,0:T(8,128)S(1)}, u32[]{:S(2)}) copy-start(f32[1,2,256,256]{3,2,1,0:T(8,128)S(1)} %reshape.268) | copy-start | bytes 1572868
  153.1 1.2 copy-start.2
  154.3 1.4 copy-start.1
  154.3 1.4 copy-start.5
